TPU v7x, 32 devices: a whole 2x2x4 slice. The times are simulated.
32 devices in a mesh: head: 4 (over y, core), ctx: 8 (over z, x).
Axes of the slice: x: 2, y: 2, z: 4, core: 2. Of those that a mesh axis runs over, the one named last changes fastest.
Arguments:
- main_queries: bfloat16 [256, 128, 192], P(None, 'head'), may hold values from -6 to 6
- main_keys: bfloat16 [8192, 128, 192], P('ctx', 'head'), may hold values from -7 to 7
- log_sums: float32 [256, 128], P(None, 'head'), may hold values from 10 to 13
- index_queries: bfloat16 [256, 64, 128], P('head'), may hold values from -2 to 2
- index_weights: bfloat16 [256, 64], P('head'), may hold values from -3 to 3
- index_keys: bfloat16 [8192, 128], P('ctx'), may hold values from -7 to 7
- loss_weights: float32 [256], P('head'), may hold values from 4 to 64
Outputs:
- query_grad: bfloat16 [256, 64, 128], P('head', 'ctx')
- weight_grad: float32 [256, 64], P('head', 'ctx')
- key_grad: bfloat16 [8192, 128], P('ctx', 'head')
All inputs are finite; a program needn't handle non-finite values.
Results may differ from a plain program's by a relative error of at most 0.023.
Values may be sent and summed in bfloat16 or wider, within the bound.
A program may use at most 128 MiB of HBM per device.

v0:
```python
import jax
import jax.numpy as jnp
from jax import lax
from jax.sharding import PartitionSpec as P

IH = 64
ID = 128


def combined_all(value, axis, join):
    pieces = jax.tree.map(lambda part: lax.all_gather(part, axis), value)
    head = jax.tree.map(lambda part: part[0], pieces)
    tail = jax.tree.map(lambda part: part[1:], pieces)
    subtotal, _ = lax.scan(lambda subtotal, slab: (join(subtotal, slab), None), head, tail)
    return subtotal


def per_device(
    main_queries, main_keys, log_sums, index_queries, index_weights, index_keys, loss_weights
):
    query_rows = index_queries.shape[0]
    key_rows = index_keys.shape[0]
    all_queries = main_queries.shape[0]
    local_heads = main_queries.shape[1]
    score_scale = main_queries.shape[2] ** (-0.5)
    block_count = all_queries // query_rows
    queries_blocks = main_queries.reshape(
        block_count, query_rows, local_heads, main_queries.shape[2]
    )
    logs_blocks = log_sums.reshape(block_count, query_rows, local_heads)

    def one_block(pieces):
        queries_block, logs_block = pieces
        scores = (
            jnp.einsum("qhd,khd->qhk", queries_block, main_keys, preferred_element_type=jnp.float32)
            * score_scale
        )
        return jnp.sum(jnp.exp(scores - logs_block[:, :, None]), axis=1)

    summed = lax.map(one_block, (queries_blocks, logs_blocks))
    probs = lax.psum_scatter(
        summed.reshape(all_queries, key_rows).astype(jnp.bfloat16),
        "head",
        scatter_dimension=0,
        tiled=True,
    ).astype(jnp.float32)
    queries_flat = index_queries.reshape(query_rows * IH, ID)
    raw_scores = jnp.dot(queries_flat, index_keys.T, preferred_element_type=jnp.float32).reshape(
        query_rows, IH, key_rows
    )
    positive = jnp.maximum(raw_scores, 0.0)
    weights_wide = index_weights.astype(jnp.float32)
    logits = jnp.sum(weights_wide[:, :, None] * positive, axis=1)
    local_top = jnp.max(logits, axis=1)
    local_mass = jnp.sum(probs, axis=1)

    def combine(former, latter):
        joint_top = jnp.maximum(former[0], latter[0])
        joint_total = former[1] * jnp.exp(former[0] - joint_top) + latter[1] * jnp.exp(
            latter[0] - joint_top
        )
        return (joint_top, joint_total, former[2] + latter[2])

    local_total = jnp.sum(jnp.exp(logits - local_top[:, None]), axis=1)
    row_top, row_total, row_mass = combined_all(
        (local_top, local_total, local_mass), "ctx", combine
    )
    soft_share = jnp.exp(logits - row_top[:, None]) / row_total[:, None]
    target = probs / row_mass[:, None]
    grad_logits = (loss_weights[:, None] * (soft_share - target)).astype(jnp.bfloat16)
    grad_wide = grad_logits.astype(jnp.float32)
    weight_term = jnp.sum(grad_wide[:, None, :] * positive, axis=2)
    gated = jnp.where(raw_scores > 0, grad_wide[:, None, :] * weights_wide[:, :, None], 0.0).astype(
        jnp.bfloat16
    )
    gated_flat = gated.reshape(query_rows * IH, key_rows)
    query_term = jnp.dot(gated_flat, index_keys, preferred_element_type=jnp.float32).reshape(
        query_rows, IH, ID
    )
    query_grad, weight_grad = (
        lax.psum_scatter(
            query_term.astype(jnp.bfloat16), "ctx", scatter_dimension=1, tiled=True
        ).astype(jnp.float32),
        lax.psum_scatter(
            weight_term.astype(jnp.bfloat16), "ctx", scatter_dimension=1, tiled=True
        ).astype(jnp.float32),
    )
    key_term = jnp.einsum("rk,rd->kd", gated_flat, queries_flat, preferred_element_type=jnp.float32)
    key_grad = lax.psum_scatter(
        key_term.astype(jnp.bfloat16), "head", scatter_dimension=1, tiled=True
    )
    return (query_grad.astype(jnp.bfloat16), weight_grad, key_grad)


def solution(mesh):
    return jax.shard_map(
        per_device,
        mesh=mesh,
        in_specs=(
            P(None, "head", None),
            P("ctx", "head", None),
            P(None, "head"),
            P("head", None, None),
            P("head", None),
            P("ctx", None),
            P("head"),
        ),
        out_specs=(P("head", "ctx", None), P("head", "ctx"), P("ctx", "head")),
        check_vma=False,
    )
```

profile of v0, /device:TPU:0, one launch (start us, length us, event | category | flops | bytes accessed | tf_op | source)
XLA Modules:
  0.0 205.3 jit_solution(16656748123852978723)
XLA Ops:
  7.2 0.0 copy-start
  7.2 0.0 reduce-scatter.6.cloned.1.call-start
  7.2 0.9 reshape.32
  8.2 7.7 %copy.13 = bf16[256,32,192]{2,1,0:T(8,128)(2,1)} copy(bf16[256,32,192]{0,2,1:T(8,128)(2,1)} %param.11) | data formatting | bytes 6291456 | tf_op args[0]
  15.9 0.0 copy-start.2
  15.9 0.0 copy-start.3
  15.9 0.0 copy-start.1
  15.9 42.1 %while.24 = (s32[]{:T(128)}, bf16[4,64,1024]{2,1,0:T(8,128)(2,1)}, bf16[4,64,32,192]{3,2,1,0:T(8,128)(2,1)}, bf16[1024,32,192]{0,2,1:T(8,128)(2,1)}, f32[4,64,32]{1,0,2:T(4,128)S(1)}, /*index=5*/s32[]{:T(128)}) while((s32[]{:T(128)}, bf16[4,64,1024]{2,1,0:T(8,128)(2,1)}, bf16[4,64,32,192]{3,2,1,0:T(8,128)(2,1)}, ...), condition=%wide.region_5.6_spmd, body=%wide.region_3.5_spmd.sunk | while | flops 811532288 | bytes 15360089 | solution.py:40
  15.9 1.3 constant_dynamic-slice_fusion.8
  17.3 8.5 %fusion.28 = bf16[64,1024]{1,0:T(8,128)(2,1)S(1)} fusion(f32[64,32]{0,1:T(8,128)S(1)} %bitcast.80, bf16[1024,32,192]{0,2,1:T(8,128)(2,1)} %get-tuple-element.212, bf16[1,64,32,192]{3,2,1,0:T(8,128)(2,1)S(1)} %constant_dynamic-slice_fusion.8), kind=kOutput, calls=%fused_computation.2.clone.1 | convolution fusion | flops 811532288 | bytes 13508608 | tf_op jit(solution)/shard_map/while/body/eval_jaxpr/qhd,khd->qhk/dot_general | solution.py:35
  25.8 0.7 bitcast_dynamic-update-slice_fusion.2
  26.5 1.3 constant_dynamic-slice_fusion.8
  27.8 8.5 %fusion.28 = bf16[64,1024]{1,0:T(8,128)(2,1)S(1)} fusion(f32[64,32]{0,1:T(8,128)S(1)} %bitcast.80, bf16[1024,32,192]{0,2,1:T(8,128)(2,1)} %get-tuple-element.212, bf16[1,64,32,192]{3,2,1,0:T(8,128)(2,1)S(1)} %constant_dynamic-slice_fusion.8), kind=kOutput, calls=%fused_computation.2.clone.1 | convolution fusion | flops 811532288 | bytes 13508608 | tf_op jit(solution)/shard_map/while/body/eval_jaxpr/qhd,khd->qhk/dot_general | solution.py:35
  36.3 0.7 bitcast_dynamic-update-slice_fusion.2
  37.0 1.3 constant_dynamic-slice_fusion.8
  38.3 8.5 %fusion.28 = bf16[64,1024]{1,0:T(8,128)(2,1)S(1)} fusion(f32[64,32]{0,1:T(8,128)S(1)} %bitcast.80, bf16[1024,32,192]{0,2,1:T(8,128)(2,1)} %get-tuple-element.212, bf16[1,64,32,192]{3,2,1,0:T(8,128)(2,1)S(1)} %constant_dynamic-slice_fusion.8), kind=kOutput, calls=%fused_computation.2.clone.1 | convolution fusion | flops 811532288 | bytes 13508608 | tf_op jit(solution)/shard_map/while/body/eval_jaxpr/qhd,khd->qhk/dot_general | solution.py:35
  46.8 0.7 bitcast_dynamic-update-slice_fusion.2
  47.5 1.3 constant_dynamic-slice_fusion.8
  48.8 8.5 %fusion.28 = bf16[64,1024]{1,0:T(8,128)(2,1)S(1)} fusion(f32[64,32]{0,1:T(8,128)S(1)} %bitcast.80, bf16[1024,32,192]{0,2,1:T(8,128)(2,1)} %get-tuple-element.212, bf16[1,64,32,192]{3,2,1,0:T(8,128)(2,1)S(1)} %constant_dynamic-slice_fusion.8), kind=kOutput, calls=%fused_computation.2.clone.1 | convolution fusion | flops 811532288 | bytes 13508608 | tf_op jit(solution)/shard_map/while/body/eval_jaxpr/qhd,khd->qhk/dot_general | solution.py:35
  57.3 0.7 bitcast_dynamic-update-slice_fusion.2
  58.0 0.0 copy-start.4
  58.0 0.0 reduce-scatter.6.cloned.1.call-update
  58.0 0.0 reduce-scatter.10.cloned.1.call-start
  58.1 0.0 copy-done.2
  58.1 0.0 copy-done.3
  58.1 0.6 fusion.20
  59.4 0.0 copy-done
  59.4 0.0 copy-done.1
  59.4 7.1 %multiply_reduce_fusion.1 = (f32[64,1024]{1,0:T(8,128)S(1)}, f32[64,64,1024]{2,1,0:T(8,128)}) fusion(f32[64,64]{1,0:T(8,128)S(1)} %convert_element_type.35, bf16[64,64,128]{2,1,0:T(8,128)(2,1)S(1)} %copy-done, bf16[1024,128]{1,0:T(8,128)(2,1)S(1)} %copy-done.1), kind=kOutput, calls=%fused_computation.19 | convolution fusion | flops 1086259200 | bytes 18366464 | tf_op jit(solution)/shard_map/dot_general | solution.py:48
  66.5 0.1 reduce_max.9
  66.6 0.2 dynamic-update-slice
  66.9 0.2 exponential_reduce_fusion
  67.1 0.2 dynamic-update-slice.1
  67.3 15.2 %reduce-scatter.6.cloned.1.call-done = bf16[64,1024]{1,0:T(8,128)(2,1)} async-done(((bf16[256,1024]{1,0:T(8,128)(2,1)}), bf16[64,1024]{1,0:T(8,128)(2,1)}) %reduce-scatter.6.cloned.1.call-update) | async-done | bytes 131088 | tf_op jit(solution)/shard_map/reduce_scatter | solution.py:41
  82.5 1.0 convert_reduce_fusion
  83.6 0.2 dynamic-update-slice.2
  83.8 21.5 %all-reduce.4 = (f32[512]{0:T(512)S(1)}, f32[512]{0:T(512)S(1)}, f32[512]{0:T(512)S(1)}) all-reduce(f32[512]{0:T(512)S(1)} %dynamic-update-slice, f32[512]{0:T(512)S(1)} %dynamic-update-slice.1, f32[512]{0:T(512)S(1)} %dynamic-update-slice.2), channel_id=2, replica_groups=mesh['head'=4,'ctx'=8] {'ctx'}, use_global_device_ids=true, to_apply=%add | all-reduce | flops 1536 | bytes 12288
  105.4 0.1 slice.27
  105.5 0.1 slice.28
  105.5 0.1 slice.29
  105.6 0.1 reshape.44
  105.7 0.1 reshape.43
  105.8 0.1 reshape.42
  105.8 0.3 while.25
  106.1 0.0 copy-done.4
  106.1 1.1 fusion.16
  107.2 7.1 %convolution_convert_fusion = bf16[64,64,128]{2,1,0:T(8,128)(2,1)S(1)} fusion(f32[64,64,1024]{2,1,0:T(8,128)} %get-tuple-element.116, f32[64,1024]{1,0:T(8,128)S(1)} %fusion.16, f32[64,64]{1,0:T(8,128)S(1)} %convert_element_type.35, bf16[1024,128]{1,0:T(8,128)(2,1)S(1)} %copy-done.1), kind=kOutput, calls=%fused_computation.20 | convolution fusion | flops 1091043328 | bytes 18366464 | tf_op jit(solution)/shard_map/dot_general | solution.py:77
  114.3 0.7 copy.17
  115.0 1.7 copy.27
  116.7 0.0 reduce-scatter.10.cloned.1.call-update
  116.7 0.2 reduce-scatter.8.cloned.1.call-start
  117.6 7.7 %fusion.9 = bf16[1024,128]{0,1:T(8,128)(2,1)} fusion(bf16[64,64,128]{2,1,0:T(8,128)(2,1)S(1)} %copy-done, f32[64,64,1024]{2,1,0:T(8,128)} %get-tuple-element.116, f32[64,1024]{1,0:T(8,128)S(1)} %fusion.16, f32[64,64]{1,0:T(8,128)S(1)} %convert_element_type.35), kind=kOutput, calls=%fused_computation.22 | convolution fusion | flops 1090650112 | bytes 18366464 | tf_op jit(solution)/shard_map/rk,rd->kd/dot_general | solution.py:88
  125.3 0.0 reduce-scatter.8.cloned.1.call-update
  125.3 7.5 %multiply_reduce_fusion = bf16[64,64]{1,0:T(8,128)(2,1)S(1)} fusion(f32[64,64,1024]{2,1,0:T(8,128)} %get-tuple-element.116, f32[64,1024]{1,0:T(8,128)S(1)} %fusion.16), kind=kLoop, calls=%fused_computation.17 | loop fusion | flops 12578816 | bytes 17047552 | tf_op jit(solution)/shard_map/reduce_sum | solution.py:72
  132.8 0.1 copy.16
  132.9 33.1 %all-reduce.3 = bf16[64,64]{0,1:T(8,128)(2,1)S(1)} all-reduce(bf16[64,64]{0,1:T(8,128)(2,1)S(1)} %copy.16), channel_id=7, replica_groups=mesh['head'=4,'ctx'=8] {'ctx'}, use_global_device_ids=true, to_apply=%region_12.13.clone | all-reduce | flops 4096 | bytes 16384
  166.1 0.6 dynamic-slice_convert_fusion
  166.7 10.0 %reduce-scatter.10.cloned.1.call-done = bf16[8,8192]{1,0:T(8,128)(2,1)} async-done(((bf16[64,8192]{1,0:T(8,128)(2,1)}), bf16[8,8192]{1,0:T(8,128)(2,1)}) %reduce-scatter.10.cloned.1.call-update) | async-done | bytes 131088
  176.6 0.9 copy.28
  177.6 0.7 copy.18
  178.3 20.4 %reduce-scatter.8.cloned.1.call-done = bf16[1024,32]{0,1:T(8,128)(2,1)} async-done(((bf16[1024,128]{0,1:T(8,128)(2,1)}), bf16[1024,32]{0,1:T(8,128)(2,1)}) %reduce-scatter.8.cloned.1.call-update) | async-done | bytes 65552 | tf_op jit(solution)/shard_map/reduce_scatter | solution.py:89
  (19 shorter events, 0.3 us)
Async XLA Ops:
  7.2 52.2 %copy-start = (bf16[64,64,128]{2,1,0:T(8,128)(2,1)S(1)}, bf16[64,64,128]{2,1,0:T(8,128)(2,1)}, u32[]{:S(2)}) copy-start(bf16[64,64,128]{2,1,0:T(8,128)(2,1)} %param.14) | copy-start | bytes 3145732
  7.2 75.4 %reduce-scatter.6.cloned.1.call-start = ((), (), s32[]{:S(2)}) async-start(), calls=%async_computation.3 | async-start | bytes 655360 | tf_op jit(solution)/shard_map/reduce_scatter | solution.py:41
  15.9 42.2 %copy-start.2 = (bf16[64,64]{1,0:T(8,128)(2,1)S(1)}, bf16[64,64]{1,0:T(8,128)(2,1)}, u32[]{:S(2)}) copy-start(bf16[64,64]{1,0:T(8,128)(2,1)} %param.15) | copy-start | bytes 24580
  15.9 42.2 %copy-start.3 = (u32[32]{0:T(128)S(1)}, u32[32]{0:T(128)}, u32[]{:S(2)}) copy-start(u32[32]{0:T(128)} %constant.34) | copy-start | bytes 388
  15.9 43.5 %copy-start.1 = (bf16[1024,128]{1,0:T(8,128)(2,1)S(1)}, bf16[1024,128]{1,0:T(8,128)(2,1)}, u32[]{:S(2)}) copy-start(bf16[1024,128]{1,0:T(8,128)(2,1)} %param.16) | copy-start | bytes 786436
  58.0 48.1 %copy-start.4 = (f32[64]{0:T(128)S(1)}, f32[64]{0:T(128)}, u32[]{:S(2)}) copy-start(f32[64]{0:T(128)} %param.17) | copy-start | bytes 772
  58.0 118.6 %reduce-scatter.10.cloned.1.call-start = ((), (), s32[]{:S(2)}) async-start(), calls=%async_computation.5 | async-start | bytes 1179648
  116.7 82.0 %reduce-scatter.8.cloned.1.call-start = ((), (), s32[]{:S(2)}) async-start(), calls=%async_computation.4 | async-start | bytes 327680 | tf_op jit(solution)/shard_map/reduce_scatter | solution.py:89
Sparse Core Ops, SparseCore 0:
  58.1 24.3 reduce-scatter.5
  116.8 59.7 reduce-scatter.9
  179.7 19.0 reduce-scatter.7
where the time goes:
time: 206 us; the launch traced here: 205 us
  matrix products  55.9 us (27%)
  blocking collectives  54.7 us (27%)
  waiting for transfers between devices  45.7 us (22%)
  local copies, waits for them, and re-layouts  22.6 us (11%)
  between operations  15.2 us (7%)
  other arithmetic  10.7 us (5%)
    unnamed x2, blocking collectives  54.7 us
    dot_general x4, matrix products, one_block(): jnp.einsum('qhd,khd->qhk', queries_block, main_keys, preferred_element_ty...  34 us
    reduce_scatter x1, waiting for transfers between devices, per_device(): lax.psum_scatter(key_term.astype(jnp.bfloat16), 'head', scatter_dimension...  20.4 us
    reduce_scatter x1, waiting for transfers between devices, per_device(): lax.psum_scatter(summed.reshape(all_queries, key_rows).astype(jnp.bfloat1...  15.2 us
    unnamed x22, local copies, waits for them, and re-layouts  13.2 us
    unnamed x4, waiting for transfers between devices  10 us
    dot_general x1, matrix products, per_device(): jnp.einsum('rk,rd->kd', gated_flat, queries_flat, preferred_element_type=...  7.68 us
    reduce_sum x1, other arithmetic, per_device(): weight_term = jnp.sum(grad_wide[:, None, :] * positive, axis=2)  7.54 us
  transfers between devices with their start and end apart: 3, of which 3 were waited for; matrix products, arithmetic and copies ran while one was open for 13% of the time, Pallas kernels for 0%

commit v1 on v0

v1 whole, which is shorter than its diff:
```python
import functools
import math

import jax
import jax.numpy as jnp
from jax import lax
from jax.experimental import pallas as pl
from jax.experimental.pallas import tpu as pltpu
from jax.sharding import PartitionSpec as P

MESH = pl.DeviceIdType.MESH
F32 = jnp.float32
BF16 = jnp.bfloat16
KEY_CHUNK = 256
LANES = 128


def column(values, index):
    lane = lax.broadcasted_iota(jnp.int32, values.shape, 1)
    return jnp.sum(jnp.where(lane == index, values, 0.0), axis=1, keepdims=True)


def kernel(
    n_head, n_ctx,
    q_ref, k_ref, ls_ref, iq_ref, iw_ref, ik_ref, lw_ref,
    out_q, out_w, out_k,
    q_raw, q_rows, k_buf, acc, group_buf, group_in, raw_buf, logits, probs, grad,
    flip, stat_buf, stat_in, m_buf, m_in, key_acc, key_buf, key_in,
    q_sem, k_sem, group_send, group_recv, stat_send, stat_recv, m_send, m_recv, key_send, key_recv,
):
    me_h, me_c = lax.axis_index("head"), lax.axis_index("ctx")
    heads, width, all_queries = q_ref.shape
    keys = k_ref.shape[2]
    rows = lw_ref.shape[1]
    index_heads = iw_ref.shape[1]
    depth = k_buf.shape[1]
    own_heads = index_heads // n_ctx
    block = own_heads * rows
    features = out_k.shape[0]
    chunks = keys // KEY_CHUNK
    scale = width ** (-0.5)
    factor = scale * math.log2(math.e)

    q_copy = pltpu.make_async_copy(q_ref, q_raw, q_sem)
    q_copy.start()
    key_copies = []
    for c in range(chunks):
        part = pl.ds(c * KEY_CHUNK, KEY_CHUNK)
        copy = pltpu.make_async_copy(
            k_ref.at[:, :, part], k_buf.at[:, pl.ds(0, width), part], k_sem.at[c]
        )
        copy.start()
        key_copies.append(copy)

    barrier = pltpu.get_barrier_semaphore()
    for o in range(1, n_head):
        pl.semaphore_signal(
            barrier, inc=1, device_id={"head": lax.rem(me_h + o, n_head)}, device_id_type=MESH
        )
    for o in range(1, n_ctx):
        pl.semaphore_signal(
            barrier, inc=1, device_id={"ctx": lax.rem(me_c + o, n_ctx)}, device_id_type=MESH
        )

    k_buf[:, width:, :] = jnp.ones((heads, depth - width, keys), BF16)
    logits[...] = jnp.zeros_like(logits)
    key_acc[...] = jnp.zeros_like(key_acc)
    q_copy.wait()

    def turn(h, carry):
        saved = ls_ref[pl.ds(h, 1), :] * (-1.0 / scale)
        high = saved.astype(BF16).astype(F32)
        middle = (saved - high).astype(BF16).astype(F32)
        low = saved - high - middle
        place = lax.broadcasted_iota(jnp.int32, (depth - width, all_queries), 0)
        extra = jnp.where(
            place == 0, high, jnp.where(place == 1, middle, jnp.where(place == 2, low, 0.0))
        ).astype(BF16)
        q_rows[h] = jnp.concatenate([q_raw[h], extra], axis=0).T
        return carry

    lax.fori_loop(0, heads, turn, 0)
    pl.semaphore_wait(barrier, n_head + n_ctx - 2)

    def group_copy(c, o):
        dest = lax.rem(me_h + o, n_head)
        return pltpu.make_async_remote_copy(
            src_ref=group_buf.at[c, pl.ds(pl.multiple_of(dest * rows, rows), rows), :],
            dst_ref=group_in.at[c, o - 1],
            send_sem=group_send.at[c, o - 1],
            recv_sem=group_recv.at[c, o - 1],
            device_id={"head": dest},
            device_id_type=MESH,
        )

    step_heads = 4 if heads % 4 == 0 else 1
    for c in range(chunks):
        key_copies[c].wait()
        acc[...] = jnp.zeros_like(acc)

        def some_heads(i, carry, c=c):
            total = None
            for u in range(step_heads):
                h = i * step_heads + u
                scores = jnp.dot(
                    q_rows[h],
                    k_buf[h, :, c * KEY_CHUNK : (c + 1) * KEY_CHUNK],
                    preferred_element_type=F32,
                )
                part = jnp.exp2(scores * factor)
                total = part if total is None else total + part
            acc[...] += total
            return carry

        lax.fori_loop(0, heads // step_heads, some_heads, 0)
        group_buf[c] = acc[...].astype(BF16)
        for o in range(1, n_head):
            group_copy(c, o).start()

    weights = iw_ref[...].astype(F32)
    tile = min(256, block)
    tile_heads = tile // rows

    def logit_step(i, carry):
        part = pl.ds(pl.multiple_of(i * tile, tile), tile)
        queries = iq_ref[part, :]
        cols = [column(weights, i * tile_heads + u) for u in range(tile_heads)]
        for c in range(chunks):
            span = slice(c * KEY_CHUNK, (c + 1) * KEY_CHUNK)
            raw = lax.dot_general(
                queries, ik_ref[span, :], (((1,), (1,)), ((), ())), preferred_element_type=F32
            )
            raw_buf[part, span] = raw.astype(BF16)
            total = logits[:, span]
            for u in range(tile_heads):
                total += cols[u] * jnp.maximum(raw[u * rows : (u + 1) * rows], 0.0)
            logits[:, span] = total
        return carry

    lax.fori_loop(0, index_heads // tile_heads, logit_step, 0)
    values = logits[...]
    top = jnp.max(values, axis=1, keepdims=True)
    total = jnp.sum(jnp.exp(values - top), axis=1, keepdims=True)

    mine = pl.ds(pl.multiple_of(me_h * rows, rows), rows)
    mass = jnp.zeros((rows, 1), F32)
    for c in range(chunks):
        summed = group_buf[c, mine, :].astype(F32)
        for o in range(1, n_head):
            group_copy(c, o).wait_recv()
            summed += group_in[c, o - 1].astype(F32)
        probs[:, c * KEY_CHUNK : (c + 1) * KEY_CHUNK] = summed
        mass += jnp.sum(summed, axis=1, keepdims=True)

    flip[...] = jnp.zeros_like(flip)
    lane = lax.broadcasted_iota(jnp.int32, (rows, LANES), 1)
    flip[0:rows, :] = jnp.where(
        lane == 0, top, jnp.where(lane == 1, total, jnp.where(lane == 2, mass, 0.0))
    )
    stat_buf[...] = flip[...].T[0:8, :]

    def stat_copy(o):
        return pltpu.make_async_remote_copy(
            src_ref=stat_buf,
            dst_ref=stat_in.at[o - 1],
            send_sem=stat_send.at[o - 1],
            recv_sem=stat_recv.at[o - 1],
            device_id={"ctx": lax.rem(me_c + o, n_ctx)},
            device_id_type=MESH,
        )

    for o in range(1, n_ctx):
        stat_copy(o).start()
    own = stat_buf[...]
    stats = [own]
    for o in range(1, n_ctx):
        stat_copy(o).wait_recv()
        stats.append(stat_in[o - 1])
    all_top = functools.reduce(jnp.maximum, [s[0:1] for s in stats])
    all_total = sum(s[1:2] * jnp.exp(s[0:1] - all_top) for s in stats)
    all_mass = sum(s[2:3] for s in stats)
    flip[0:1, :] = all_top
    flip[1:2, :] = 1.0 / all_total
    flip[2:3, :] = 1.0 / all_mass
    flip[3:4, 0:rows] = lw_ref[...]
    back = flip[...].T[0:rows, :]
    top, per_total, per_mass, loss = (back[:, i : i + 1] for i in range(4))
    soft = jnp.exp(logits[...] - top) * per_total
    grad[...] = (loss * (soft - probs[...] * per_mass)).astype(BF16)

    def m_copy(o):
        dest = lax.rem(me_c + o + 1, n_ctx)
        return pltpu.make_async_remote_copy(
            src_ref=m_buf.at[pl.ds(pl.multiple_of(dest * block, block), block), :],
            dst_ref=m_in.at[o],
            send_sem=m_send.at[o],
            recv_sem=m_recv.at[o],
            device_id={"ctx": dest},
            device_id_type=MESH,
        )

    def grad_step(o, carry):
        dest = lax.rem(me_c + o + 1, n_ctx)
        for v in range(block // tile):
            start = pl.multiple_of(dest * block + v * tile, tile)
            part = pl.ds(start, tile)
            queries = iq_ref[part, :].astype(F32)
            first = dest * own_heads + v * tile_heads
            scaled = jnp.concatenate(
                [
                    queries[u * rows : (u + 1) * rows] * column(weights, first + u)
                    for u in range(tile_heads)
                ],
                axis=0,
            )
            gated = jnp.concatenate(
                [
                    jnp.where(
                        raw_buf[pl.ds(start + u * rows, rows), :] > 0, grad[...], jnp.zeros((), BF16)
                    )
                    for u in range(tile_heads)
                ],
                axis=0,
            )
            m_buf[part, :] = jnp.dot(gated, ik_ref[...], preferred_element_type=F32).astype(BF16)
            key_acc[...] += jnp.dot(scaled.T.astype(BF16), gated, preferred_element_type=F32)

        @pl.when(o < n_ctx - 1)
        def _():
            m_copy(o).start()

        return carry

    lax.fori_loop(0, n_ctx, grad_step, 0)

    key_buf[...] = key_acc[...].astype(BF16)

    def key_copy(o):
        dest = lax.rem(me_h + o, n_head)
        return pltpu.make_async_remote_copy(
            src_ref=key_buf.at[pl.ds(pl.multiple_of(dest * features, features), features), :],
            dst_ref=key_in.at[o - 1],
            send_sem=key_send.at[o - 1],
            recv_sem=key_recv.at[o - 1],
            device_id={"head": dest},
            device_id_type=MESH,
        )

    for o in range(1, n_head):
        key_copy(o).start()
    key_total = key_buf[pl.ds(pl.multiple_of(me_h * features, features), features), :].astype(F32)
    for o in range(1, n_head):
        key_copy(o).wait_recv()
        key_total += key_in[o - 1].astype(F32)
    out_k[...] = key_total.astype(BF16)

    own_rows = pl.ds(pl.multiple_of(me_c * block, block), block)
    m_total = m_buf[own_rows, :].astype(F32)
    for o in range(n_ctx - 1):
        m_copy(o).wait_recv()
        m_total += m_in[o].astype(F32)
    dots = iq_ref[own_rows, :].astype(F32) * m_total
    place = lax.broadcasted_iota(jnp.int32, (rows, own_heads), 1)
    weight_total = jnp.zeros((rows, own_heads), F32)
    for u in range(own_heads):
        span = slice(u * rows, (u + 1) * rows)
        col = column(weights, me_c * own_heads + u)
        out_q[u] = (m_total[span] * col).astype(BF16)
        weight_total = jnp.where(
            place == u, jnp.sum(dots[span], axis=1, keepdims=True), weight_total
        )
    out_w[...] = weight_total

    for c in range(chunks):
        for o in range(1, n_head):
            group_copy(c, o).wait_send()
    for o in range(1, n_ctx):
        stat_copy(o).wait_send()
    for o in range(n_ctx - 1):
        m_copy(o).wait_send()
    for o in range(1, n_head):
        key_copy(o).wait_send()


def per_device(
    n_head, n_ctx,
    main_queries, main_keys, log_sums, index_queries, index_weights, index_keys, loss_weights,
):
    all_queries, heads, width = main_queries.shape
    keys = main_keys.shape[0]
    rows, index_heads, size = index_queries.shape
    own_heads = index_heads // n_ctx
    features = size // n_head
    depth = (width + 16 + LANES - 1) // LANES * LANES
    chunks = keys // KEY_CHUNK
    flat = rows * index_heads
    queries = index_queries.transpose(1, 0, 2).reshape(flat, size)
    vmem = pl.BlockSpec(memory_space=pltpu.VMEM)
    hbm = pl.BlockSpec(memory_space=pl.ANY)
    dma = pltpu.SemaphoreType.DMA
    query_grad, weight_grad, key_grad = pl.pallas_call(
        functools.partial(kernel, n_head, n_ctx),
        out_shape=(
            jax.ShapeDtypeStruct((own_heads, rows, size), BF16),
            jax.ShapeDtypeStruct((rows, own_heads), F32),
            jax.ShapeDtypeStruct((features, keys), BF16),
        ),
        in_specs=[hbm, hbm, vmem, vmem, vmem, vmem, vmem],
        out_specs=(vmem, vmem, vmem),
        scratch_shapes=[
            pltpu.VMEM((heads, width, all_queries), BF16),
            pltpu.VMEM((heads, all_queries, depth), BF16),
            pltpu.VMEM((heads, depth, keys), BF16),
            pltpu.VMEM((all_queries, KEY_CHUNK), F32),
            pltpu.VMEM((chunks, all_queries, KEY_CHUNK), BF16),
            pltpu.VMEM((chunks, n_head - 1, rows, KEY_CHUNK), BF16),
            pltpu.VMEM((flat, keys), BF16),
            pltpu.VMEM((rows, keys), F32),
            pltpu.VMEM((rows, keys), F32),
            pltpu.VMEM((rows, keys), BF16),
            pltpu.VMEM((LANES, LANES), F32),
            pltpu.VMEM((8, LANES), F32),
            pltpu.VMEM((n_ctx - 1, 8, LANES), F32),
            pltpu.VMEM((flat, size), BF16),
            pltpu.VMEM((n_ctx - 1, own_heads * rows, size), BF16),
            pltpu.VMEM((size, keys), F32),
            pltpu.VMEM((size, keys), BF16),
            pltpu.VMEM((n_head - 1, features, keys), BF16),
            dma, dma((chunks,)),
            dma((chunks, n_head - 1)), dma((chunks, n_head - 1)),
            dma((n_ctx - 1,)), dma((n_ctx - 1,)),
            dma((n_ctx - 1,)), dma((n_ctx - 1,)),
            dma((n_head - 1,)), dma((n_head - 1,)),
        ],
        compiler_params=pltpu.CompilerParams(
            collective_id=0, has_side_effects=True, vmem_limit_bytes=56 * 1024 * 1024
        ),
        name="indexer_backward",
    )(
        main_queries.transpose(1, 2, 0),
        main_keys.transpose(1, 2, 0),
        log_sums.T,
        queries,
        index_weights,
        index_keys,
        loss_weights.reshape(1, rows),
    )
    return query_grad.transpose(1, 0, 2), weight_grad, key_grad.T


def solution(mesh):
    return jax.shard_map(
        functools.partial(per_device, mesh.shape["head"], mesh.shape["ctx"]),
        mesh=mesh,
        in_specs=(
            P(None, "head", None),
            P("ctx", "head", None),
            P(None, "head"),
            P("head", None, None),
            P("head", None),
            P("ctx", None),
            P("head"),
        ),
        out_specs=(P("head", "ctx", None), P("head", "ctx"), P("ctx", "head")),
        check_vma=False,
    )
```

time: 206 us -> 61.8 us (0.30)
  the two profiles are of different devices: /device:TPU:0 before, /device:TPU:11 now
where the time goes in v1:
time: 61.8 us; the launch traced here: 61.5 us
  Pallas kernels  53.4 us (86%)
  local copies, waits for them, and re-layouts  7.43 us (12%)
  between operations  0.64 us (1%)
    pallas_call x1, Pallas kernels, per_device(): pl.pallas_call(functools.partial(kernel, n_head, n_ctx), out_shape=(jax.S...  53.4 us
    unnamed x3, local copies, waits for them, and re-layouts  4.54 us
    transpose x1, local copies, waits for them, and re-layouts, per_device(): queries = index_queries.transpose(1, 0, 2).reshape(flat, size)  2.89 us

profile of v1, /device:TPU:11, one launch (start us, length us, event | category | flops | bytes accessed | tf_op | source)
XLA Modules:
  0.0 61.5 jit_solution(8118308053399773295)
XLA Ops:
  0.6 2.9 %copy.10 = bf16[64,64,128]{2,1,0:T(8,128)(2,1)} copy(bf16[64,64,128]{2,0,1:T(8,128)(2,1)} %bitcast.11) | data formatting | bytes 2097152 | tf_op jit(solution)/shard_map/transpose | solution.py:297
  3.5 53.4 %indexer_backward.1 = (bf16[8,64,128]{2,1,0:T(8,128)(2,1)}, f32[64,8]{1,0:T(8,128)}, bf16[32,1024]{1,0:T(8,128)(2,1)}) custom-call(bf16[32,192,256]{2,1,0:T(8,128)(2,1)} %bitcast.10, bf16[32,192,1024]{2,1,0:T(8,128)(2,1)} %bitcast.8, f32[32,256]{1,0:T(8,128)} %bitcast.14, bf16[4096,128]{1,0:T(8,128)(2,1)} %bitcast.9, bf16[64,64]{1,0:T(8,128)(2,1)} %iw_ref.1, ...), custom_call_target="tpu_custom_call" | custom-call | tf_op jit(solution)/shard_map/indexer_backward/pallas_call | solution.py:301
  56.9 1.6 %copy.11 = bf16[64,8,128]{2,1,0:T(8,128)(2,1)} copy(bf16[64,8,128]{2,0,1:T(8,128)(2,1)} %bitcast.12) | data formatting | bytes 262144
  58.6 1.4 %copy.12 = f32[64,8]{0,1:T(8,128)} copy(f32[64,8]{1,0:T(8,128)} %get-tuple-element.10) | data formatting | bytes 4096
  60.0 1.5 %copy.14 = bf16[1024,32]{0,1:T(8,128)(2,1)} copy(bf16[1024,32]{0,1:T(8,128)(2,1)} %bitcast.13) | data formatting | bytes 131072

commit v2 on v1

--- a/solution.py
+++ b/solution.py
@@ -22,11 +22,11 @@
 
 def kernel(
     n_head, n_ctx,
-    q_ref, k_ref, ls_ref, iq_ref, iw_ref, ik_ref, lw_ref,
+    q_ref, k_ref, ls_ref, iq_in, iw_ref, ik_ref, lw_ref,
     out_q, out_w, out_k,
     q_raw, q_rows, k_buf, acc, group_buf, group_in, raw_buf, logits, probs, grad,
-    flip, stat_buf, stat_in, m_buf, m_in, key_acc, key_buf, key_in,
-    q_sem, k_sem, group_send, group_recv, stat_send, stat_recv, m_send, m_recv, key_send, key_recv,
+    flip, stat_buf, stat_in, iq_ref, m_buf, p_in, m_in, key_acc, key_buf, key_in,
+    q_sem, k_sem, group_send, group_recv, stat_send, stat_recv, p_send, p_recv, m_send, m_recv, key_send, key_recv,
 ):
     me_h, me_c = lax.axis_index("head"), lax.axis_index("ctx")
     heads, width, all_queries = q_ref.shape
@@ -37,6 +37,7 @@
     own_heads = index_heads // n_ctx
     block = own_heads * rows
     features = out_k.shape[0]
+    size = ik_ref.shape[1]
     chunks = keys // KEY_CHUNK
     scale = width ** (-0.5)
     factor = scale * math.log2(math.e)
@@ -65,6 +66,9 @@
     k_buf[:, width:, :] = jnp.ones((heads, depth - width, keys), BF16)
     logits[...] = jnp.zeros_like(logits)
     key_acc[...] = jnp.zeros_like(key_acc)
+    iq_ref[...] = (
+        jnp.swapaxes(iq_in[...].astype(F32), 0, 1).reshape(iq_ref.shape).astype(BF16)
+    )
     q_copy.wait()
 
     def turn(h, carry):
@@ -92,30 +96,6 @@
             device_id={"head": dest},
             device_id_type=MESH,
         )
-
-    step_heads = 4 if heads % 4 == 0 else 1
-    for c in range(chunks):
-        key_copies[c].wait()
-        acc[...] = jnp.zeros_like(acc)
-
-        def some_heads(i, carry, c=c):
-            total = None
-            for u in range(step_heads):
-                h = i * step_heads + u
-                scores = jnp.dot(
-                    q_rows[h],
-                    k_buf[h, :, c * KEY_CHUNK : (c + 1) * KEY_CHUNK],
-                    preferred_element_type=F32,
-                )
-                part = jnp.exp2(scores * factor)
-                total = part if total is None else total + part
-            acc[...] += total
-            return carry
-
-        lax.fori_loop(0, heads // step_heads, some_heads, 0)
-        group_buf[c] = acc[...].astype(BF16)
-        for o in range(1, n_head):
-            group_copy(c, o).start()
 
     weights = iw_ref[...].astype(F32)
     tile = min(256, block)
@@ -137,7 +117,34 @@
             logits[:, span] = total
         return carry
 
-    lax.fori_loop(0, index_heads // tile_heads, logit_step, 0)
+    logit_steps = index_heads // tile_heads
+    lax.fori_loop(0, logit_steps // 2, logit_step, 0)
+
+    step_heads = 4 if heads % 4 == 0 else 1
+    for c in range(chunks):
+        key_copies[c].wait()
+        acc[...] = jnp.zeros_like(acc)
+
+        def some_heads(i, carry, c=c):
+            total = None
+            for u in range(step_heads):
+                h = i * step_heads + u
+                scores = jnp.dot(
+                    q_rows[h],
+                    k_buf[h, :, c * KEY_CHUNK : (c + 1) * KEY_CHUNK],
+                    preferred_element_type=F32,
+                )
+                part = jnp.exp2(scores * factor)
+                total = part if total is None else total + part
+            acc[...] += total
+            return carry
+
+        lax.fori_loop(0, heads // step_heads, some_heads, 0)
+        group_buf[c] = acc[...].astype(BF16)
+        for o in range(1, n_head):
+            group_copy(c, o).start()
+
+    lax.fori_loop(logit_steps // 2, logit_steps, logit_step, 0)
     values = logits[...]
     top = jnp.max(values, axis=1, keepdims=True)
     total = jnp.sum(jnp.exp(values - top), axis=1, keepdims=True)
@@ -188,19 +195,41 @@
     soft = jnp.exp(logits[...] - top) * per_total
     grad[...] = (loss * (soft - probs[...] * per_mass)).astype(BF16)
 
-    def m_copy(o):
-        dest = lax.rem(me_c + o + 1, n_ctx)
+    pairs = n_ctx // 2
+    side = lax.rem(me_c, 2)
+    pair = me_c // 2
+
+    def rows_of(i, other):
+        dest = lax.rem(pair + i + 1, pairs) * 2 + (1 - side if other else side)
+        return dest, pl.ds(pl.multiple_of(dest * block, block), block)
+
+    def p_copy(i):
         return pltpu.make_async_remote_copy(
-            src_ref=m_buf.at[pl.ds(pl.multiple_of(dest * block, block), block), :],
-            dst_ref=m_in.at[o],
-            send_sem=m_send.at[o],
-            recv_sem=m_recv.at[o],
+            src_ref=m_buf.at[rows_of(i, True)[1], :],
+            dst_ref=p_in.at[i],
+            send_sem=p_send.at[i],
+            recv_sem=p_recv.at[i],
+            device_id={"ctx": pair * 2 + 1 - side},
+            device_id_type=MESH,
+        )
+
+    def m_copy(i):
+        dest, part = rows_of(i, False)
+        return pltpu.make_async_remote_copy(
+            src_ref=m_buf.at[part, :],
+            dst_ref=m_in.at[i],
+            send_sem=m_send.at[i],
+            recv_sem=m_recv.at[i],
             device_id={"ctx": dest},
             device_id_type=MESH,
         )
 
-    def grad_step(o, carry):
-        dest = lax.rem(me_c + o + 1, n_ctx)
+    def join(i):
+        part = rows_of(i, False)[1]
+        p_copy(i).wait_recv()
+        m_buf[part, :] = (m_buf[part, :].astype(F32) + p_in[i].astype(F32)).astype(BF16)
+
+    def grad_block(dest):
         for v in range(block // tile):
             start = pl.multiple_of(dest * block + v * tile, tile)
             part = pl.ds(start, tile)
@@ -225,13 +254,23 @@
             m_buf[part, :] = jnp.dot(gated, ik_ref[...], preferred_element_type=F32).astype(BF16)
             key_acc[...] += jnp.dot(scaled.T.astype(BF16), gated, preferred_element_type=F32)
 
-        @pl.when(o < n_ctx - 1)
+    def other_side(i, carry):
+        grad_block(rows_of(i, True)[0])
+        p_copy(i).start()
+        return carry
+
+    def own_side(i, carry):
+        grad_block(rows_of(i, False)[0])
+
+        @pl.when(jnp.logical_and(i == 0, pairs > 1))
         def _():
-            m_copy(o).start()
+            join(i)
+            m_copy(i).start()
 
         return carry
 
-    lax.fori_loop(0, n_ctx, grad_step, 0)
+    lax.fori_loop(0, pairs, other_side, 0)
+    lax.fori_loop(0, pairs, own_side, 0)
 
     key_buf[...] = key_acc[...].astype(BF16)
 
@@ -248,6 +287,10 @@
 
     for o in range(1, n_head):
         key_copy(o).start()
+    for i in range(1, pairs):
+        join(i)
+        if i < pairs - 1:
+            m_copy(i).start()
     key_total = key_buf[pl.ds(pl.multiple_of(me_h * features, features), features), :].astype(F32)
     for o in range(1, n_head):
         key_copy(o).wait_recv()
@@ -256,30 +299,42 @@
 
     own_rows = pl.ds(pl.multiple_of(me_c * block, block), block)
     m_total = m_buf[own_rows, :].astype(F32)
-    for o in range(n_ctx - 1):
-        m_copy(o).wait_recv()
-        m_total += m_in[o].astype(F32)
+    for i in range(pairs - 1):
+        m_copy(i).wait_recv()
+        m_total += m_in[i].astype(F32)
     dots = iq_ref[own_rows, :].astype(F32) * m_total
-    place = lax.broadcasted_iota(jnp.int32, (rows, own_heads), 1)
-    weight_total = jnp.zeros((rows, own_heads), F32)
+    flip[...] = jnp.zeros_like(flip)
+    weight_total = flip[0:rows, :]
+    grads = []
     for u in range(own_heads):
         span = slice(u * rows, (u + 1) * rows)
-        col = column(weights, me_c * own_heads + u)
-        out_q[u] = (m_total[span] * col).astype(BF16)
+        grads.append(m_total[span] * column(weights, me_c * own_heads + u))
         weight_total = jnp.where(
-            place == u, jnp.sum(dots[span], axis=1, keepdims=True), weight_total
-        )
-    out_w[...] = weight_total
+            lane == u, jnp.sum(dots[span], axis=1, keepdims=True), weight_total
+        )
+    out_q[...] = jnp.swapaxes(
+        jnp.concatenate(grads, axis=0).reshape(own_heads, rows, size), 0, 1
+    ).astype(BF16)
+    flip[0:rows, :] = weight_total
+    out_w[...] = flip[...].T[0:own_heads, 0:rows]
 
     for c in range(chunks):
         for o in range(1, n_head):
             group_copy(c, o).wait_send()
     for o in range(1, n_ctx):
         stat_copy(o).wait_send()
-    for o in range(n_ctx - 1):
-        m_copy(o).wait_send()
+    for i in range(pairs):
+        p_copy(i).wait_send()
+    for i in range(pairs - 1):
+        m_copy(i).wait_send()
     for o in range(1, n_head):
         key_copy(o).wait_send()
+
+
+def hand_out(q_in, w_in, k_in, q_out, w_out, k_out):
+    q_out[...] = q_in[...]
+    w_out[...] = w_in[...]
+    k_out[...] = k_in[...]
 
 
 def per_device(
@@ -294,15 +349,15 @@
     depth = (width + 16 + LANES - 1) // LANES * LANES
     chunks = keys // KEY_CHUNK
     flat = rows * index_heads
-    queries = index_queries.transpose(1, 0, 2).reshape(flat, size)
+    pairs = n_ctx // 2
     vmem = pl.BlockSpec(memory_space=pltpu.VMEM)
     hbm = pl.BlockSpec(memory_space=pl.ANY)
     dma = pltpu.SemaphoreType.DMA
     query_grad, weight_grad, key_grad = pl.pallas_call(
         functools.partial(kernel, n_head, n_ctx),
         out_shape=(
-            jax.ShapeDtypeStruct((own_heads, rows, size), BF16),
-            jax.ShapeDtypeStruct((rows, own_heads), F32),
+            jax.ShapeDtypeStruct((rows, own_heads, size), BF16),
+            jax.ShapeDtypeStruct((own_heads, rows), F32),
             jax.ShapeDtypeStruct((features, keys), BF16),
         ),
         in_specs=[hbm, hbm, vmem, vmem, vmem, vmem, vmem],
@@ -322,14 +377,17 @@
             pltpu.VMEM((8, LANES), F32),
             pltpu.VMEM((n_ctx - 1, 8, LANES), F32),
             pltpu.VMEM((flat, size), BF16),
-            pltpu.VMEM((n_ctx - 1, own_heads * rows, size), BF16),
+            pltpu.VMEM((flat, size), BF16),
+            pltpu.VMEM((pairs, own_heads * rows, size), BF16),
+            pltpu.VMEM((pairs - 1, own_heads * rows, size), BF16),
             pltpu.VMEM((size, keys), F32),
             pltpu.VMEM((size, keys), BF16),
             pltpu.VMEM((n_head - 1, features, keys), BF16),
             dma, dma((chunks,)),
             dma((chunks, n_head - 1)), dma((chunks, n_head - 1)),
             dma((n_ctx - 1,)), dma((n_ctx - 1,)),
-            dma((n_ctx - 1,)), dma((n_ctx - 1,)),
+            dma((pairs,)), dma((pairs,)),
+            dma((pairs - 1,)), dma((pairs - 1,)),
             dma((n_head - 1,)), dma((n_head - 1,)),
         ],
         compiler_params=pltpu.CompilerParams(
@@ -340,12 +398,20 @@
         main_queries.transpose(1, 2, 0),
         main_keys.transpose(1, 2, 0),
         log_sums.T,
-        queries,
+        index_queries,
         index_weights,
         index_keys,
         loss_weights.reshape(1, rows),
     )
-    return query_grad.transpose(1, 0, 2), weight_grad, key_grad.T
+    results = (query_grad, weight_grad, key_grad)
+    query_grad, weight_grad, key_grad = pl.pallas_call(
+        hand_out,
+        out_shape=tuple(jax.ShapeDtypeStruct(x.shape, x.dtype) for x in results),
+        in_specs=[vmem] * 3,
+        out_specs=(vmem,) * 3,
+        name="hand_out",
+    )(*results)
+    return query_grad, weight_grad.T, key_grad.T
 
 
 def solution(mesh):

time: 61.8 us -> 49.9 us (0.81)
  the two profiles are of different devices: /device:TPU:11 before, /device:TPU:0 now
where the time goes in v2:
time: 49.9 us; the launch traced here: 49.7 us
  Pallas kernels  49.1 us (98%)
  between operations  0.64 us (1%)
    pallas_call x1, Pallas kernels, per_device(): pl.pallas_call(functools.partial(kernel, n_head, n_ctx), out_shape=(jax.S...  47.5 us
    pallas_call x1, Pallas kernels, per_device(): pl.pallas_call(hand_out, out_shape=tuple((jax.ShapeDtypeStruct(x.shape, x...  1.59 us

profile of v2, /device:TPU:0, one launch (start us, length us, event | category | flops | bytes accessed | tf_op | source)
XLA Modules:
  0.0 49.7 jit_solution(1864450158015606569)
XLA Ops:
  0.6 47.5 %indexer_backward.1 = (bf16[64,8,128]{2,1,0:T(8,128)(2,1)}, f32[8,64]{1,0:T(8,128)}, bf16[32,1024]{1,0:T(8,128)(2,1)}) custom-call(bf16[32,192,256]{2,1,0:T(8,128)(2,1)} %bitcast.7, bf16[32,192,1024]{2,1,0:T(8,128)(2,1)} %bitcast.6, f32[32,256]{1,0:T(8,128)} %bitcast.8, bf16[64,64,128]{2,1,0:T(8,128)(2,1)} %iq_in.1, bf16[64,64]{1,0:T(8,128)(2,1)} %iw_ref.1, ...), custom_call_target="tpu_custom_call" | custom-call | tf_op jit(solution)/shard_map/indexer_backward/pallas_call | solution.py:356
  48.1 1.6 %hand_out.1 = (bf16[64,8,128]{2,1,0:T(8,128)(2,1)}, f32[8,64]{1,0:T(8,128)}, bf16[32,1024]{1,0:T(8,128)(2,1)}) custom-call(bf16[64,8,128]{2,1,0:T(8,128)(2,1)} %get-tuple-element.9.q_in, f32[8,64]{1,0:T(8,128)} %get-tuple-element.10.w_in, bf16[32,1024]{1,0:T(8,128)(2,1)} %get-tuple-element.11.k_in), custom_call_target="tpu_custom_call" | custom-call | tf_op jit(solution)/shard_map/hand_out/pallas_call | solution.py:407
